TPU v7x, 32 devices: a whole 2x2x4 slice. The times are simulated.
32 devices in a mesh: section: 2 (over x), ctx: 16 (over z, y, core).
Axes of the slice: x: 2, y: 2, z: 4, core: 2. Of those that a mesh axis runs over, the one named last changes fastest.
Arguments:
- activations: bfloat16 [2, 24, 8192], P('section'), may hold values from -6 to 6
- act_frames: int32 [2, 24], replicated, may hold values from 0 to 191
- fresh_batch: bfloat16 [24, 8192], replicated, may hold values from -6 to 6
- fresh_frames: int32 [24], replicated, may hold values from 0 to 191
- norm_gain: float32 [2, 8192], P('section'), may hold values from 0.1 to 1.9
- cached_keys: bfloat16 [2, 12288, 1024], P('section', 'ctx'), may hold values from -64 to 64
- cached_values: bfloat16 [2, 12288, 1024], P('section', 'ctx'), may hold values from -6 to 6
- key_frames: int32 [12288], P('ctx'), may hold values from 0 to 191, never falling along the last dimension, each value on 1 to 128 neighbouring positions
Outputs:
- result: bfloat16 [2, 24, 8192], P('section')
Inputs may be any that keep to these rules, and one draw needn't show every extreme that they name: `key_frames`: frame indices never fall along the clip, and every frame of 0 to 191 holds at least one token.
All inputs are finite; a program needn't handle non-finite values.
Results may differ from a plain program's by a relative error of at most 0.019.
Values may be sent and summed in bfloat16 or wider, within the bound.
No kernel may reach another device: no remote copies, remote signals or barrier semaphores. Data moves between devices by JAX's collectives and lax.ppermute only.
A program may use at most 64 MiB of HBM per device.

v0:
```python
import jax
import jax.numpy as jnp
from jax import lax
from jax.sharding import PartitionSpec as P

HEADS = 64
HD = 128


epsilon = 1e-05
masked_score = -1e30


def passed_along(block, axis, distance):
    devices = range(lax.axis_size(axis))
    route = [(i - distance, i) for i in devices if i - distance in devices]
    return lax.ppermute(block, axis, route)


def partial_terms(
    hidden, frames, norm_scale, key_cache, value_cache, key_frames, head_count, head_size
):
    token_count = hidden.shape[0]
    kv_heads = key_cache.shape[1] // head_size
    widened = hidden.astype(jnp.float32)
    per_head = widened.reshape(token_count, head_count, head_size)
    scale_heads = norm_scale.reshape(head_count, head_size)
    queries = (
        per_head
        * lax.rsqrt(jnp.mean(per_head * per_head, axis=-1, keepdims=True) + epsilon)
        * scale_heads[None]
    ).astype(jnp.bfloat16)
    grouped = queries.reshape(token_count, kv_heads, head_count // kv_heads, head_size)
    key_rows = key_cache.reshape(-1, kv_heads, head_size)
    value_rows = value_cache.reshape(-1, kv_heads, head_size)
    scores = jnp.einsum(
        "tkgd,jkd->tkgj", grouped, key_rows, preferred_element_type=jnp.float32
    ) * head_size ** (-0.5)
    visible = key_frames[None, None, None, :] <= frames[:, None, None, None]
    scores = jnp.where(visible, scores, masked_score)
    block_max = jnp.max(scores, axis=-1)
    probabilities = jnp.where(visible, jnp.exp(scores - block_max[..., None]), 0.0).astype(
        jnp.bfloat16
    )
    totals = jnp.sum(probabilities.astype(jnp.float32), axis=-1)
    weighted = jnp.einsum(
        "tkgj,jkd->tkgd", probabilities, value_rows, preferred_element_type=jnp.float32
    )
    partials = (
        block_max.reshape(token_count, head_count),
        totals.reshape(token_count, head_count),
        weighted.reshape(token_count, head_count, head_size),
    )
    return (widened, partials)


def layer(hidden, frames, norm_scale, key_cache, value_cache, key_frames):
    widened, partials = partial_terms(
        hidden, frames, norm_scale, key_cache, value_cache, key_frames, HEADS, HD
    )
    overall = lax.pmax(partials[0], "ctx")
    factors = jnp.exp(partials[0] - overall)
    denominator, numerator = lax.psum(
        (factors * partials[1], factors[..., None] * partials[2]), "ctx"
    )
    attended = (numerator / denominator[..., None]).reshape(widened.shape)
    return (widened + attended).astype(jnp.bfloat16)


def body(
    activations,
    act_frames,
    fresh_batch,
    fresh_frames,
    norm_gain,
    cached_keys,
    cached_values,
    key_frames,
):
    section_index = lax.axis_index("section")
    own_frames = lax.dynamic_index_in_dim(act_frames, section_index, 0, keepdims=False)
    first_out = layer(
        activations[0], own_frames, norm_gain[0], cached_keys[0], cached_values[0], key_frames
    )
    handed = passed_along(first_out, "section", 1)
    prior_frames = lax.dynamic_index_in_dim(
        act_frames, jnp.maximum(section_index - 1, 0), 0, keepdims=False
    )
    incoming = jnp.where(section_index == 0, fresh_batch, handed)
    frames_in = jnp.where(section_index == 0, fresh_frames, prior_frames)
    second = layer(incoming, frames_in, norm_gain[0], cached_keys[0], cached_values[0], key_frames)
    return second[None]


def solution(mesh):
    placed = (
        P("section", None, None),
        P(),
        P(),
        P(),
        P("section", None),
        P("section", "ctx", None),
        P("section", "ctx", None),
        P("ctx"),
    )
    return jax.shard_map(
        body, mesh=mesh, in_specs=placed, out_specs=P("section", None, None), check_vma=False
    )
```

profile of v0, /device:TPU:0, one launch (start us, length us, event | category | flops | bytes accessed | tf_op | source)
XLA Modules:
  0.0 356.5 jit_solution(12016801486262911132)
XLA Ops:
  6.5 1.0 convert_bitcast_fusion
  7.6 1.1 fusion.24
  8.6 0.1 copy.63
  8.8 0.1 copy.64
  9.0 0.3 reduce_sum.36
  9.3 0.1 copy.31
  9.4 0.1 copy.32
  9.5 1.9 copy.65
  11.3 3.0 copy.66
  14.4 0.1 broadcast_compare_fusion
  14.5 3.4 bitcast_reduce_fusion.1
  17.9 0.1 copy.35
  18.0 63.0 %pmax.14 = f32[24,64]{0,1:T(8,128)S(1)} all-reduce(f32[24,64]{0,1:T(8,128)S(1)} %bitcast.105), channel_id=1, replica_groups=mesh['section'=2,'ctx'=16] {'ctx'}, use_global_device_ids=true, to_apply=%region_2.3 | all-reduce | flops 1536 | bytes 12288 | tf_op jit(solution)/shard_map/pmax | solution.py:61
  80.9 4.2 %convert_reduce_fusion.1 = f32[24,8,8]{2,0,1:T(8,128)S(1)} fusion(f32[24,8,8]{2,0,1:T(8,128)S(1)} %get-tuple-element.13, f32[8,24,8,768]{3,2,1,0:T(8,128)} %get-tuple-element.14, pred[24,768]{1,0:T(8,128)(4,1)S(1)} %get-tuple-element.12), kind=kLoop, calls=%fused_computation.12 | loop fusion | flops 8256000 | bytes 4749312 | tf_op jit(solution)/shard_map/reduce_sum | solution.py:45
  85.2 3.0 fusion.14
  88.2 0.1 copy.39
  88.3 0.1 copy.36
  88.4 1.2 bitcast_multiply_fusion.1
  89.5 0.0 all-reduce.3.cloned.1.call-update
  89.6 0.0 all-reduce.5.cloned.1.call-start
  89.6 57.7 %psum.29 = f32[24,64]{0,1:T(8,128)S(1)} all-reduce(f32[24,64]{0,1:T(8,128)S(1)} %get-tuple-element.9), channel_id=1, replica_groups=mesh['section'=2,'ctx'=16] {'ctx'}, use_global_device_ids=true, to_apply=%region_5.6 | all-reduce | flops 1536 | bytes 12288 | tf_op jit(solution)/shard_map/psum | solution.py:63
  147.3 0.1 copy.40
  147.4 31.7 %all-reduce.3.cloned.1.call-done = f32[24,64,128]{2,1,0:T(8,128)} async-done(((f32[24,64,128]{2,1,0:T(8,128)}), f32[24,64,128]{2,1,0:T(8,128)}) %all-reduce.3.cloned.1.call-update) | async-done | bytes 786448 | tf_op jit(solution)/shard_map/psum | solution.py:63
  179.1 1.4 broadcast_divide_fusion.1
  180.5 0.5 fusion.23
  181.0 3.6 %collective-permute-start = (bf16[24,8192]{1,0:T(8,128)(2,1)S(1)}, bf16[24,8192]{1,0:T(8,128)(2,1)S(1)}, u32[]{:S(2)}, u32[]{:S(2)}) collective-permute-start(bf16[24,8192]{1,0:T(8,128)(2,1)S(1)} %fusion.23), channel_id=1, source_target_pairs={{0,16},{1,17},{2,18},{3,19},{4,20},{5,21},{6,22},{7,23},{8,24},{9,... | collective-permute-start | bytes 1179656 | tf_op jit(solution)/shard_map/ppermute | solution.py:17
  184.5 7.3 %collective-permute-done = bf16[24,8192]{1,0:T(8,128)(2,1)S(1)} collective-permute-done((bf16[24,8192]{1,0:T(8,128)(2,1)S(1)}, bf16[24,8192]{1,0:T(8,128)(2,1)S(1)}, u32[]{:S(2)}, u32[]{:S(2)}) %collective-permute-start) | collective-permute-done | bytes 393248 | tf_op jit(solution)/shard_map/ppermute | solution.py:17
  191.8 0.1 fusion.20
  191.9 0.1 copy.69
  192.1 0.3 reduce_sum.38
  192.4 0.1 copy.41
  192.5 0.1 copy.42
  192.6 0.1 convert_bitcast_fusion.2
  192.6 0.1 copy.68
  192.8 1.4 bitcast_reduce_fusion
  194.1 1.5 fusion.17
  195.7 1.8 convert_reduce_fusion
  197.5 0.1 copy.45
  197.5 0.1 copy.49
  197.6 57.6 %pmax.15 = f32[24,64]{0,1:T(8,128)S(1)} all-reduce(f32[24,64]{0,1:T(8,128)S(1)} %bitcast.106), channel_id=1, replica_groups=mesh['section'=2,'ctx'=16] {'ctx'}, use_global_device_ids=true, to_apply=%region_8.9 | all-reduce | flops 1536 | bytes 12288 | tf_op jit(solution)/shard_map/pmax | solution.py:61
  255.3 0.1 copy.46
  255.3 1.2 bitcast_multiply_fusion
  256.5 0.0 all-reduce.5.cloned.1.call-update
  256.6 57.9 %psum.31 = f32[24,64]{0,1:T(8,128)S(1)} all-reduce(f32[24,64]{0,1:T(8,128)S(1)} %get-tuple-element.5), channel_id=1, replica_groups=mesh['section'=2,'ctx'=16] {'ctx'}, use_global_device_ids=true, to_apply=%region_11.12 | all-reduce | flops 1536 | bytes 12288 | tf_op jit(solution)/shard_map/psum | solution.py:63
  314.4 0.1 copy.50
  314.5 32.6 %all-reduce.5.cloned.1.call-done = f32[24,64,128]{2,1,0:T(8,128)} async-done(((f32[24,64,128]{2,1,0:T(8,128)}), f32[24,64,128]{2,1,0:T(8,128)}) %all-reduce.5.cloned.1.call-update) | async-done | bytes 786448 | tf_op jit(solution)/shard_map/psum | solution.py:63
  347.1 1.4 broadcast_divide_fusion
  348.5 1.2 fusion.31
  (23 shorter events, 0.1 us)
Async XLA Ops:
  6.5 172.5 %all-reduce.3.cloned.1.call-start = ((), (), s32[]{:S(2)}) async-start(), calls=%async_computation | async-start | bytes 1572864 | tf_op jit(solution)/shard_map/psum | solution.py:63
  8.8 5.6 %copy-start.7 = (s32[2,24]{1,0:T(2,128)S(1)}, s32[2,24]{1,0:T(2,128)}, u32[]{:S(2)}) copy-start(s32[2,24]{1,0:T(2,128)} %param.9) | copy-start | bytes 580
  8.8 5.6 %copy-start.6 = (s32[24]{0:T(128)S(1)}, s32[24]{0:T(128)}, u32[]{:S(2)}) copy-start(s32[24]{0:T(128)} %param.11) | copy-start | bytes 292
  8.8 5.6 %copy-start.5 = (s32[768]{0:T(1024)S(1)}, s32[768]{0:T(1024)}, u32[]{:S(2)}) copy-start(s32[768]{0:T(1024)} %param.15) | copy-start | bytes 9220
  8.8 5.7 %copy-start.4 = (f32[1,8192]{1,0:T(1,128)S(1)}, f32[1,8192]{1,0:T(1,128)}, u32[]{:S(2)}) copy-start(f32[1,8192]{1,0:T(1,128)} %param.12) | copy-start | bytes 98308
  80.9 4.2 %copy-start = (f32[8,24,8,768]{3,2,1,0:T(8,128)S(1)}, f32[8,24,8,768]{3,2,1,0:T(8,128)}, u32[]{:S(2)}) copy-start(f32[8,24,8,768]{3,2,1,0:T(8,128)} %get-tuple-element.14) | copy-start | bytes 14155780
  85.2 95.3 %copy-start.1 = (bf16[1,24,8192]{2,1,0:T(8,128)(2,1)S(1)}, bf16[1,24,8192]{2,1,0:T(8,128)(2,1)}, u32[]{:S(2)}) copy-start(bf16[1,24,8192]{2,1,0:T(8,128)(2,1)} %param.8) | copy-start | bytes 1179652
  88.2 103.7 %copy-start.3 = (bf16[24,8192]{1,0:T(8,128)(2,1)S(1)}, bf16[24,8192]{1,0:T(8,128)(2,1)}, u32[]{:S(2)}) copy-start(bf16[24,8192]{1,0:T(8,128)(2,1)} %param.10) | copy-start | bytes 1179652
  89.6 257.5 %all-reduce.5.cloned.1.call-start = ((), (), s32[]{:S(2)}) async-start(), calls=%async_computation.1 | async-start | bytes 1572864 | tf_op jit(solution)/shard_map/psum | solution.py:63
  181.0 10.9 %collective-permute-start = (bf16[24,8192]{1,0:T(8,128)(2,1)S(1)}, bf16[24,8192]{1,0:T(8,128)(2,1)S(1)}, u32[]{:S(2)}, u32[]{:S(2)}) collective-permute-start(bf16[24,8192]{1,0:T(8,128)(2,1)S(1)} %fusion.23), channel_id=1, source_target_pairs={{0,16},{1,17},{2,18},{3,19},{4,20},{5,21},{6,22},{7,23},{8,24},{9,... | collective-permute-start | bytes 1179656 | tf_op jit(solution)/shard_map/ppermute | solution.py:17
  192.6 1.5 copy-start.2
Sparse Core Ops, SparseCore 0:
  89.7 89.3 all-reduce.2
  256.7 90.3 all-reduce.4
where the time goes:
time: 357 us
  blocking collectives  236 us (66%)
  waiting for transfers between devices  71.6 us (20%)
  other arithmetic  15.8 us (4%)
  between operations  13.7 us (4%)
  matrix products  9.26 us (3%)
  local copies, waits for them, and re-layouts  6.4 us (2%)
  starting transfers between devices  3.62 us (1%)
    pmax x2, blocking collectives, layer(): overall = lax.pmax(partials[0], 'ctx')  121 us
    psum x2, blocking collectives, layer(): lax.psum((factors * partials[1], factors[..., None] * partials[2]), 'ctx')  116 us
    psum x2, waiting for transfers between devices, layer(): lax.psum((factors * partials[1], factors[..., None] * partials[2]), 'ctx')  64.3 us
    ppermute x1, waiting for transfers between devices, passed_along(): return lax.ppermute(block, axis, route)  7.28 us
  transfers between devices with their start and end apart: 3, of which 3 were waited for; matrix products, arithmetic and copies ran while one was open for 0% of the time, Pallas kernels for 0%

commit v1 on v0

v1 whole, which is shorter than its diff:
```python
import functools
import math

import jax
import jax.numpy as jnp
from jax import lax
from jax.experimental import pallas as pl
from jax.experimental.pallas import tpu as pltpu
from jax.sharding import PartitionSpec as P

HEADS = 64
HD = 128
PAIR = 2
INNER = 2
BLOCKS = 4
STAT_ROWS = 16
HIDDEN = -(2.0**100)
SCALE = HD**-0.5 * math.log2(math.e)
MIB = 1 << 20

epsilon = 1e-05

WHOLE = pl.BlockSpec(memory_space=pltpu.VMEM)
IN_HBM = pl.BlockSpec(memory_space=pltpu.HBM)


def in_hbm(*arrays):
    return [pltpu.with_memory_space_constraint(a, pltpu.HBM) for a in arrays]


def in_vmem(*arrays):
    return [pltpu.with_memory_space_constraint(a, pltpu.VMEM) for a in arrays]


def place_here():
    return lax.axis_index("ctx") % PAIR


def inner_here():
    return lax.axis_index("ctx") // PAIR % INNER


def outer_here():
    return lax.axis_index("ctx") // (PAIR * INNER)


def in_first_section():
    return lax.axis_index("section") == 0


def swapped(block):
    return lax.ppermute(block, "ctx", [(i, i ^ 1) for i in range(lax.axis_size("ctx"))])


def beside(i, step):
    block = INNER * PAIR
    return i // block * block + (i + PAIR * step) % block


def from_inner(block):
    return lax.ppermute(block, "ctx", [(i, beside(i, 1)) for i in range(lax.axis_size("ctx"))])


def from_outer(blocks):
    size = lax.axis_size("ctx")
    return [
        lax.ppermute(block, "ctx", [(i, (i + INNER * PAIR * (d + 1)) % size) for i in range(size)])
        for d, block in enumerate(blocks)
    ]


def from_section_before(block, step):
    sections, size = lax.axis_size("section"), lax.axis_size("ctx")
    route = [
        (s * size + i, (s + 1) * size + beside(i, step))
        for s in range(sections - 1)
        for i in range(size)
    ]
    return lax.ppermute(block, ("section", "ctx"), route)


def head_rows(block):
    return jnp.concatenate(
        [block[:, at : at + HD] for at in range(0, block.shape[1], HD)], axis=0
    )


def row_of(ref):
    return jnp.concatenate([ref[i : i + 1] for i in range(ref.shape[0])], axis=1)


def columns_of(index, ref, width):
    return ref.at[:, pl.ds(pl.multiple_of(index * width, HD), width)]


def on_diagonal(rows):
    shape = (rows, HD)
    return lax.broadcasted_iota(jnp.int32, shape, 0) == lax.broadcasted_iota(jnp.int32, shape, 1)


def queries_of(x, gain):
    rows = head_rows(x.astype(jnp.float32))
    gain = head_rows(jnp.broadcast_to(gain, x.shape))
    norm = lax.rsqrt(jnp.mean(rows * rows, axis=-1, keepdims=True) + epsilon)
    return (rows * norm * gain).astype(jnp.bfloat16)


def bias_of(keys_ref, frames):
    length = keys_ref.shape[0] - STAT_ROWS
    width = keys_ref.shape[1]
    rows = -(-length // width)
    tail = keys_ref[length:].astype(jnp.float32)
    key_frames = jnp.concatenate([tail[i : i + 1] for i in range(rows)], axis=1)[:, :length]
    return jnp.where(key_frames <= frames, 0.0, HIDDEN)[None]


def scores(queries, key_block, bias):
    count, keys, tokens = queries.shape[0], key_block.shape[0], bias.shape[1]
    raw = lax.dot_general(
        queries, key_block, (((1,), (1,)), ((), ())), preferred_element_type=jnp.float32
    )
    raw = raw.reshape(count // tokens, tokens, keys) * SCALE + bias
    return raw.reshape(count, keys)


def top_of(raw):
    top = jnp.max(raw, axis=-1, keepdims=True)
    return top.astype(jnp.bfloat16).astype(jnp.float32)


def weigh(raw, top, value_block):
    probs = jnp.exp2(raw - top).astype(jnp.bfloat16)
    ones = jnp.ones((value_block.shape[0], HD), jnp.bfloat16)
    return jnp.dot(
        probs, jnp.concatenate([value_block, ones], axis=1), preferred_element_type=jnp.float32
    )


def groups_of(count):
    groups = -(-count // HD)
    held = count // groups
    return [slice(c * held, (c + 1) * held) for c in range(groups)]


def write_chunk(out_ref, weighted, tops, totals):
    count = weighted.shape[0]
    line = lax.broadcasted_iota(jnp.int32, (STAT_ROWS, HD), 0)
    stats = jnp.zeros((STAT_ROWS, HD), jnp.float32)
    for c, (top, total) in enumerate(zip(tops, totals)):
        high = total.astype(jnp.bfloat16).astype(jnp.float32)
        for n, row in enumerate((top, high, total - high)):
            stats = jnp.where(line == 3 * c + n, row, stats)
    out_ref[:count] = weighted.astype(jnp.bfloat16)
    out_ref[count:] = stats.astype(jnp.bfloat16)


def write_sums(out_ref, weighted, top, total):
    groups = groups_of(weighted.shape[0])
    diagonal = on_diagonal(groups[0].stop)

    def rows(column):
        column = jnp.broadcast_to(column, weighted.shape)
        return [
            jnp.sum(jnp.where(diagonal, column[group], 0.0), axis=0, keepdims=True)
            for group in groups
        ]

    write_chunk(out_ref, weighted, rows(top), rows(total))


def joined(parts, normed):
    count = parts[0].shape[0] - STAT_ROWS
    groups = groups_of(count)
    diagonal = on_diagonal(groups[0].stop)
    stats = [part[count:].astype(jnp.float32) for part in parts]
    values, tops, totals = [], [], []
    for c, group in enumerate(groups):
        points = [s[3 * c : 3 * c + 1] for s in stats]
        top = functools.reduce(jnp.maximum, points)
        factors = [jnp.exp2(point - top) for point in points]
        total = sum(
            f * (s[3 * c + 1 : 3 * c + 2] + s[3 * c + 2 : 3 * c + 3])
            for f, s in zip(factors, stats)
        )
        if normed:
            inverse = 1.0 / total
            factors = [f * inverse for f in factors]
        value = 0.0
        for factor, part in zip(factors, parts):
            weight = jnp.where(diagonal, factor, 0.0)[:, : group.stop - group.start]
            high = weight.astype(jnp.bfloat16)
            low = (weight - high.astype(jnp.float32)).astype(jnp.bfloat16)
            for term in (high, low):
                value = value + jnp.dot(term, part[group], preferred_element_type=jnp.float32)
        values.append(value)
        tops.append(top)
        totals.append(total)
    return jnp.concatenate(values, axis=0), tops, totals


def stage(sources, own_ref, given_ref, staged_ref, gift_ref, sems, gift_sems, tail):
    length, width = staged_ref.shape
    half, step = width // PAIR, length // BLOCKS
    copies = []
    for b in range(BLOCKS):
        rows = pl.ds(b * step, step)
        copies.append(pltpu.make_async_copy(sources.at[rows], staged_ref.at[rows], sems.at[b]))
        copies[-1].start()
    yield
    if tail is not None:
        gift_ref[length:] = tail()
        own_ref[length:] = tail()
    place = place_here()
    gifts = []
    for b, copy in enumerate(copies):
        copy.wait()
        rows = pl.ds(b * step, step)
        gift_ref[rows] = columns_of(1 - place, staged_ref.at[rows], half)[...]
        own_ref[rows] = columns_of(place, staged_ref.at[rows], half)[...]
        if b == BLOCKS - 1:
            rows = pl.ds(b * step, gift_ref.shape[0] - b * step)
        gifts.append(pltpu.make_async_copy(gift_ref.at[rows], given_ref.at[rows], gift_sems.at[b]))
        gifts[-1].start()
    yield
    for gift in gifts:
        gift.wait()
    yield


def load_keys_kernel(
    key_frames_in, keys_in, own_ref, given_ref,
    key_frames_ref, staged_ref, gift_ref, sems, gift_sems, small_sem,
):
    length, half = staged_ref.shape[0], own_ref.shape[1]
    small = pltpu.make_async_copy(key_frames_in, key_frames_ref, small_sem)
    small.start()

    def tail():
        row = row_of(key_frames_ref).astype(jnp.float32)
        lines = -(-length // half)
        row = jnp.concatenate([row, jnp.zeros((1, lines * half - length), jnp.float32)], axis=1)
        line = lax.broadcasted_iota(jnp.int32, (STAT_ROWS, half), 0)
        lower = jnp.zeros((STAT_ROWS, half), jnp.float32)
        for n in range(lines):
            lower = jnp.where(line == n, row[:, n * half : (n + 1) * half], lower)
        return lower.astype(jnp.bfloat16)

    steps = stage(keys_in, own_ref, given_ref, staged_ref, gift_ref, sems, gift_sems, tail)
    next(steps)
    small.wait()
    next(steps)
    next(steps)


def load_keys(key_frames, keys):
    length, width = keys.shape
    shape = (length + STAT_ROWS, width // PAIR)
    return pl.pallas_call(
        load_keys_kernel,
        in_specs=[IN_HBM] * 2,
        out_specs=[WHOLE, IN_HBM],
        out_shape=[pltpu.VMEM(shape, keys.dtype), pltpu.HBM(shape, keys.dtype)],
        scratch_shapes=[
            pltpu.VMEM(key_frames.shape, key_frames.dtype),
            pltpu.VMEM((length, width), keys.dtype),
            pltpu.VMEM(shape, keys.dtype),
            pltpu.SemaphoreType.DMA((BLOCKS,)),
            pltpu.SemaphoreType.DMA((BLOCKS,)),
            pltpu.SemaphoreType.DMA,
        ],
        cost_estimate=pl.CostEstimate(
            flops=0, bytes_accessed=2 * length * width, transcendentals=0
        ),
        compiler_params=pltpu.CompilerParams(vmem_limit_bytes=16 * MIB),
        name="load_keys",
    )(*in_hbm(key_frames, keys))


def load_values_kernel(
    act_frames_in, fresh_frames_in, values_in, batch_in, fresh_in, gain_in,
    own_ref, given_ref, batches_ref, gain_ref, frames_ref,
    act_frames_ref, fresh_frames_ref, staged_ref, gift_ref, sems, gift_sems, small_sems,
):
    place, half = place_here(), gain_ref.shape[1]
    small = [
        (act_frames_in, act_frames_ref),
        (fresh_frames_in, fresh_frames_ref),
        (columns_of(place, batch_in, half), batches_ref.at[0]),
        (columns_of(place, gain_in, half), gain_ref),
        (columns_of(place, fresh_in, half), batches_ref.at[1]),
    ]
    small = [pltpu.make_async_copy(a, b, small_sems.at[n]) for n, (a, b) in enumerate(small)]
    for copy in small[:2]:
        copy.start()
    steps = stage(values_in, own_ref, given_ref, staged_ref, gift_ref, sems, gift_sems, None)
    next(steps)
    for copy in small[2:]:
        copy.start()
    for copy in small[:2]:
        copy.wait()

    tokens = frames_ref.shape[1]
    section = lax.axis_index("section")
    own_row = act_frames_ref[pl.ds(section, 1), :].astype(jnp.float32)
    prior_row = act_frames_ref[pl.ds(jnp.maximum(section - 1, 0), 1), :].astype(jnp.float32)
    fresh_row = fresh_frames_ref[...].astype(jnp.float32)
    next_row = jnp.where(in_first_section(), fresh_row, prior_row)
    shape = (tokens, tokens)
    diagonal = lax.broadcasted_iota(jnp.int32, shape, 0) == lax.broadcasted_iota(jnp.int32, shape, 1)
    for tick, row in enumerate((own_row, next_row)):
        column = jnp.sum(jnp.where(diagonal, row, 0.0), axis=1, keepdims=True)
        frames_ref[tick] = jnp.broadcast_to(column, (tokens, HD))

    next(steps)
    for copy in small[2:]:
        copy.wait()
    next(steps)


def load_values(act_frames, fresh_frames, values, batch, fresh, gain):
    length, width = values.shape
    tokens, model = batch.shape
    half = model // PAIR
    shape = (length, width // PAIR)
    return pl.pallas_call(
        load_values_kernel,
        in_specs=[IN_HBM] * 6,
        out_specs=[WHOLE, IN_HBM] + [WHOLE] * 3,
        out_shape=[
            pltpu.VMEM(shape, values.dtype),
            pltpu.HBM(shape, values.dtype),
            pltpu.VMEM((2, tokens, half), batch.dtype),
            pltpu.VMEM((1, half), gain.dtype),
            pltpu.VMEM((2, tokens, HD), jnp.float32),
        ],
        scratch_shapes=[
            pltpu.VMEM(act_frames.shape, act_frames.dtype),
            pltpu.VMEM(fresh_frames.shape, fresh_frames.dtype),
            pltpu.VMEM((length, width), values.dtype),
            pltpu.VMEM(shape, values.dtype),
            pltpu.SemaphoreType.DMA((BLOCKS,)),
            pltpu.SemaphoreType.DMA((BLOCKS,)),
            pltpu.SemaphoreType.DMA((5,)),
        ],
        cost_estimate=pl.CostEstimate(
            flops=0, bytes_accessed=2 * length * width, transcendentals=0
        ),
        compiler_params=pltpu.CompilerParams(vmem_limit_bytes=16 * MIB),
        name="load_values",
    )(*in_hbm(act_frames, fresh_frames, values, batch, fresh, gain))


def begin_kernel(
    gain_ref, frames_ref, batches_ref, keys_ref, values_ref,
    queries_ref, sums_ref, stats_ref, share_ref,
):
    length = values_ref.shape[0]
    kv_here = values_ref.shape[1] // HD
    count, width = queries_ref.shape[0] // kv_here, gain_ref.shape[1] // kv_here
    bias = bias_of(keys_ref, frames_ref[0, :, :1])
    share_ref[...] = columns_of(outer_here(), batches_ref.at[0], share_ref.shape[1])[...]
    for g in range(kv_here):
        rows, columns = slice(g * count, (g + 1) * count), slice(g * width, (g + 1) * width)
        block = slice(g * HD, (g + 1) * HD)
        queries = queries_of(batches_ref[0, :, columns], gain_ref[:, columns])
        queries_ref[rows] = queries
        raw = scores(queries, keys_ref[:length, block], bias)
        top = top_of(raw)
        both = weigh(raw, top, values_ref[:, block])
        sums_ref[rows] = both[:, :HD]
        lane = lax.broadcasted_iota(jnp.int32, (count, HD), 1)
        stats_ref[rows] = jnp.where(lane < HD // 2, top, both[:, HD:])


def begin(gain, frames, batches, keys, values):
    length, width = values.shape
    _, tokens, half = batches.shape
    queries = HEADS // PAIR * tokens
    return pl.pallas_call(
        begin_kernel,
        in_specs=[WHOLE] * 5,
        out_specs=[WHOLE] * 4,
        out_shape=[
            jax.ShapeDtypeStruct((queries, HD), jnp.bfloat16),
            jax.ShapeDtypeStruct((queries, HD), jnp.float32),
            jax.ShapeDtypeStruct((queries, HD), jnp.float32),
            jax.ShapeDtypeStruct((tokens, half * HD // width), batches.dtype),
        ],
        cost_estimate=pl.CostEstimate(
            flops=2 * queries * length * 3 * HD,
            bytes_accessed=4 * length * width,
            transcendentals=queries * length,
        ),
        compiler_params=pltpu.CompilerParams(vmem_limit_bytes=16 * MIB),
        name="begin",
    )(*in_vmem(gain, frames, batches, keys, values))


def chunk_shapes(count):
    shape = jax.ShapeDtypeStruct((count + STAT_ROWS, HD), jnp.bfloat16)
    return shape


def finish_kernel(
    frames_ref, queries_ref, sums_ref, stats_ref, keys_ref, values_ref, *out_refs
):
    length = values_ref.shape[0]
    kv_here, outer = len(out_refs), outer_here()
    count = queries_ref.shape[0] // kv_here
    bias = bias_of(keys_ref, frames_ref[0, :, :1])
    for d, out_ref in enumerate(out_refs):
        g = (outer + d) % kv_here
        rows = pl.ds(pl.multiple_of(g * count, count), count)
        raw = scores(queries_ref[rows], columns_of(g, keys_ref.at[:length], HD)[...], bias)
        stats = stats_ref[rows]
        before, totals = stats[:, :1], stats[:, HD // 2 : HD // 2 + 1]
        top = jnp.maximum(before, top_of(raw))
        factor = jnp.exp2(before - top)
        both = weigh(raw, top, columns_of(g, values_ref, HD)[...])
        weighted = both[:, :HD] + sums_ref[rows] * factor
        write_sums(out_ref, weighted, top, both[:, HD:] + totals * factor)


def finish(frames, queries, sums, stats, keys, values):
    length, width = values.shape
    count, kv_here = queries.shape[0], width // HD
    return pl.pallas_call(
        finish_kernel,
        in_specs=[WHOLE] * 6,
        out_specs=[WHOLE] * kv_here,
        out_shape=[chunk_shapes(count // kv_here)] * kv_here,
        cost_estimate=pl.CostEstimate(
            flops=2 * count * length * 3 * HD,
            bytes_accessed=4 * length * width,
            transcendentals=count * length,
        ),
        compiler_params=pltpu.CompilerParams(vmem_limit_bytes=16 * MIB),
        name="finish",
    )(*in_vmem(frames, queries, sums, stats, keys, values))


def partials_kernel(gain_ref, frames_ref, batches_ref, *refs):
    kv_refs, refs = (refs[0:2], refs[2:4]), refs[4:]
    kv_here = len(refs) // 2
    handed_refs, out_refs = refs[:kv_here], refs[kv_here:]
    length, outer, first = kv_refs[0][1].shape[0], outer_here(), in_first_section()
    width = gain_ref.shape[1] // kv_here
    frames = frames_ref[1, :, :1]
    biases = [bias_of(keys_ref, frames) for keys_ref, _ in kv_refs]
    for d, out_ref in enumerate(out_refs):
        g = (outer + d) % kv_here
        fresh = columns_of(g, batches_ref.at[1], width)[...].astype(jnp.float32)
        handed = handed_refs[(kv_here - d) % kv_here][...].astype(jnp.float32)
        x = jnp.where(first, fresh, handed)
        queries = queries_of(x, columns_of(g, gain_ref, width)[...])
        raws = [
            scores(queries, columns_of(g, keys_ref.at[:length], HD)[...], bias)
            for (keys_ref, _), bias in zip(kv_refs, biases)
        ]
        top = functools.reduce(jnp.maximum, [top_of(raw) for raw in raws])
        both = sum(
            weigh(raw, top, columns_of(g, values_ref, HD)[...])
            for raw, (_, values_ref) in zip(raws, kv_refs)
        )
        write_sums(out_ref, both[:, :HD], top, both[:, HD:])


def partials(gain, frames, batches, own, got, handed):
    length, width = own[1].shape
    _, tokens, half = batches.shape
    queries = HEADS // PAIR * tokens
    kv_here = width // HD
    return pl.pallas_call(
        partials_kernel,
        in_specs=[WHOLE] * (7 + kv_here),
        out_specs=[WHOLE] * kv_here,
        out_shape=[chunk_shapes(queries // kv_here)] * kv_here,
        cost_estimate=pl.CostEstimate(
            flops=2 * queries * PAIR * length * 3 * HD,
            bytes_accessed=8 * length * width,
            transcendentals=queries * PAIR * length,
        ),
        compiler_params=pltpu.CompilerParams(vmem_limit_bytes=16 * MIB),
        name="partials",
    )(*in_vmem(gain, frames, batches, *own, *got, *handed))


def merge_kernel(*refs):
    *parts, out_ref = refs
    write_chunk(out_ref, *joined(parts, False))


def merge(parts):
    return pl.pallas_call(
        merge_kernel,
        in_specs=[WHOLE] * len(parts),
        out_specs=WHOLE,
        out_shape=jax.ShapeDtypeStruct(parts[0].shape, parts[0].dtype),
        compiler_params=pltpu.CompilerParams(vmem_limit_bytes=8 * MIB),
        name="merge",
    )(*in_vmem(*parts))


def combined(one_ref, two_ref, x, out_ref):
    one, two = one_ref[...].astype(jnp.float32), two_ref[...].astype(jnp.float32)
    here = inner_here() == 0
    parts = [jnp.where(here, one, two), jnp.where(here, two, one)]
    attended, _, _ = joined([part.astype(jnp.bfloat16) for part in parts], True)
    total = head_rows(x.astype(jnp.float32)) + attended
    tokens = out_ref.shape[0]
    for h in range(total.shape[0] // tokens):
        piece = total[h * tokens : (h + 1) * tokens]
        out_ref[:, h * HD : (h + 1) * HD] = piece.astype(jnp.bfloat16)


def combine_kernel(one_ref, two_ref, share_ref, out_ref):
    combined(one_ref, two_ref, share_ref[...], out_ref)


def combine_last_kernel(one_ref, two_ref, batches_ref, handed_ref, out_ref):
    fresh = columns_of(outer_here(), batches_ref.at[1], out_ref.shape[1])[...]
    x = jnp.where(
        in_first_section(), fresh.astype(jnp.float32), handed_ref[...].astype(jnp.float32)
    )
    combined(one_ref, two_ref, x, out_ref)


def combine(kernel, one, two, *rest):
    return pl.pallas_call(
        kernel,
        in_specs=[WHOLE] * (2 + len(rest)),
        out_specs=WHOLE,
        out_shape=jax.ShapeDtypeStruct(rest[-1].shape, jnp.bfloat16),
        compiler_params=pltpu.CompilerParams(vmem_limit_bytes=8 * MIB),
        name="combine",
    )(*in_vmem(one, two, *rest))


def assemble_kernel(*refs):
    *pieces, out_ref = refs
    outers = len(pieces) // PAIR
    width = pieces[0].shape[1]
    for n, refs in enumerate((pieces[:outers], pieces[outers:])):
        place = (place_here() + n) % PAIR
        for d, ref in enumerate(refs):
            index = place * outers + (outer_here() + outers - d) % outers
            columns_of(index, out_ref, width)[...] = ref[...]


def assemble(mine, others):
    tokens, width = mine[0].shape
    pieces = [*mine, *others]
    return pl.pallas_call(
        assemble_kernel,
        in_specs=[WHOLE] * len(pieces),
        out_specs=WHOLE,
        out_shape=jax.ShapeDtypeStruct((tokens, len(pieces) * width), jnp.bfloat16),
        compiler_params=pltpu.CompilerParams(vmem_limit_bytes=8 * MIB),
        name="assemble",
    )(*in_vmem(*pieces))


def body(
    activations,
    act_frames,
    fresh_batch,
    fresh_frames,
    norm_gain,
    cached_keys,
    cached_values,
    key_frames,
):
    own_keys, given_keys = load_keys(key_frames.reshape(-1, HD), cached_keys[0])
    got_keys = swapped(given_keys)
    own_values, given_values, batches, gain, frames = load_values(
        act_frames, fresh_frames[None], cached_values[0], activations[0], fresh_batch, norm_gain
    )
    got_values = swapped(given_values)
    own, got = (own_keys, own_values), (got_keys, got_values)

    *terms, share = begin(gain, frames, batches, *own)
    share = from_section_before(share, 0)
    chunk, *others = finish(frames, *terms, *got)
    chunk = merge([chunk, *from_outer(others)])
    one, two = [from_section_before(chunk, step) for step in range(INNER)]
    handed = combine(combine_kernel, one, two, share)
    handed = [handed, *from_outer([handed] * (lax.axis_size("ctx") // (INNER * PAIR) - 1))]

    chunk, *others = partials(gain, frames, batches, own, got, handed)
    chunk = merge([chunk, *from_outer(others)])
    share = combine(combine_last_kernel, chunk, from_inner(chunk), batches, handed[0])
    mine = [share, *from_outer([share] * len(others))]
    return assemble(mine, [swapped(piece) for piece in mine])[None]


def solution(mesh):
    placed = (
        P("section", None, None),
        P(),
        P(),
        P(),
        P("section", None),
        P("section", "ctx", None),
        P("section", "ctx", None),
        P("ctx"),
    )
    return jax.shard_map(
        body, mesh=mesh, in_specs=placed, out_specs=P("section", None, None), check_vma=False
    )
```

time: 357 us -> 61.9 us (0.17)
  blocking collectives: 236 us -> 0 us
  waiting for transfers between devices: 71.6 us -> 23.9 us
  starting transfers between devices: 3.62 us -> 26.6 us
  other arithmetic: 15.8 us -> 0 us
  between operations: 13.7 us -> 0.12 us
  Pallas kernels: 0 us -> 11.1 us
  matrix products: 9.26 us -> 0 us
  local copies, waits for them, and re-layouts: 6.4 us -> 0 us
    pmax x2 -> x0, blocking collectives: 121 us -> none  [layer(): overall = lax.pmax(partials[0], 'ctx')]
    psum x2 -> x0, blocking collectives: 116 us -> none  [layer(): lax.psum((factors * partials[1], factors[..., None] * partials[2]), 'ctx')]
    psum x2 -> x0, waiting for transfers between devices: 64.3 us -> none  [layer(): lax.psum((factors * partials[1], factors[..., None] * partials[2]), 'ctx')]
    ppermute x1 -> x22, starting transfers between devices: 3.58 us -> 26.6 us  [the longest x12 18.4 us: from_outer(): lax.ppermute(block, 'ctx', [(i, (i + INNER * PAIR * (d + 1)) % size) for...]
    ppermute x1 -> x22, waiting for transfers between devices: 7.28 us -> 23.9 us  [the longest x12 16.1 us: from_outer(): lax.ppermute(block, 'ctx', [(i, (i + INNER * PAIR * (d + 1)) % size) for...]
    pallas_call x0 -> x10, Pallas kernels: none -> 11.1 us  [the longest x1 2.18 us: load_values(): pl.pallas_call(load_values_kernel, in_specs=[IN_HBM] * 6, out_specs=[WHOL...]
    dot_general x4 -> x0, matrix products: 9.26 us -> none  [the longest x2 4.74 us: partial_terms(): jnp.einsum('tkgd,jkd->tkgj', grouped, key_rows, preferred_element_type=jn...]
    reduce_sum x4 -> x0, other arithmetic: 6.56 us -> none  [the longest x2 6.01 us: partial_terms(): totals = jnp.sum(probabilities.astype(jnp.float32), axis=-1)]
  transfers between devices with their start and end apart: 3 -> 22, of which waited for: 3 -> 16; matrix products, arithmetic and copies ran while one was open for 0% -> 0% of each run, Pallas kernels for 0% -> 6%
where the time goes in v1:
time: 61.9 us; the launch traced here: 61.7 us
  starting transfers between devices  26.6 us (43%)
  waiting for transfers between devices  23.9 us (39%)
  Pallas kernels  11.1 us (18%)
    ppermute x12, starting transfers between devices, from_outer(): lax.ppermute(block, 'ctx', [(i, (i + INNER * PAIR * (d + 1)) % size) for...  18.4 us
    ppermute x12, waiting for transfers between devices, from_outer(): lax.ppermute(block, 'ctx', [(i, (i + INNER * PAIR * (d + 1)) % size) for...  16.1 us
    ppermute x3, starting transfers between devices, from_section_before(): return lax.ppermute(block, ('section', 'ctx'), route)  6.94 us
    ppermute x1, waiting for transfers between devices, from_inner(): lax.ppermute(block, 'ctx', [(i, beside(i, 1)) for i in range(lax.axis_siz...  3.57 us
    ppermute x6, waiting for transfers between devices, swapped(): lax.ppermute(block, 'ctx', [(i, i ^ 1) for i in range(lax.axis_size('ctx'...  2.41 us
    pallas_call x1, Pallas kernels, load_values(): pl.pallas_call(load_values_kernel, in_specs=[IN_HBM] * 6, out_specs=[WHOL...  2.18 us
    pallas_call x1, Pallas kernels, partials(): pl.pallas_call(partials_kernel, in_specs=[WHOLE] * (7 + kv_here), out_spe...  2.17 us
    pallas_call x1, Pallas kernels, load_keys(): pl.pallas_call(load_keys_kernel, in_specs=[IN_HBM] * 2, out_specs=[WHOLE,...  2.14 us
  transfers between devices with their start and end apart: 22, of which 16 were waited for; matrix products, arithmetic and copies ran while one was open for 0% of the time, Pallas kernels for 6%

profile of v1, /device:TPU:0, one launch (start us, length us, event | category | flops | bytes accessed | tf_op | source)
XLA Modules:
  0.0 61.7 jit_solution(3366101323742123640)
XLA Ops:
  0.0 2.1 %load_keys.1 = (bf16[784,512]{1,0:T(8,128)(2,1)S(1)}, bf16[784,512]{1,0:T(8,128)(2,1)}) custom-call(s32[6,128]{1,0:T(8,128)} %bitcast.9, bf16[768,1024]{1,0:T(8,128)(2,1)} %bitcast.6), custom_call_target="tpu_custom_call" | custom-call | bytes 1572864 | tf_op jit(solution)/shard_map/load_keys/pallas_call | solution.py:258
  2.1 0.5 collective-permute-start
  2.7 2.2 %load_values.1 = (bf16[768,512]{1,0:T(8,128)(2,1)S(1)}, bf16[768,512]{1,0:T(8,128)(2,1)}, bf16[2,24,4096]{2,1,0:T(8,128)(2,1)S(1)}, f32[1,4096]{1,0:T(1,128)S(1)}, f32[2,24,128]{2,1,0:T(8,128)S(1)}) custom-call(s32[2,24]{1,0:T(2,128)} %act_frames_in.1, s32[1,24]{1,0:T(1,128)} %bitcast.10, bf16[768,1024]{1,0:T(8,128)(2,1)} %bitcast.7, ...), custom_call_target="tpu_custom_call" | custom-call | bytes 1572864 | tf_op jit(solution)/shard_map/load_values/pallas_call | solution.py:325
  4.9 0.1 collective-permute-start.1
  5.0 1.2 %begin.1 = (bf16[768,128]{1,0:T(8,128)(2,1)S(1)}, f32[768,128]{1,0:T(8,128)S(1)}, f32[768,128]{1,0:T(8,128)S(1)}, bf16[24,1024]{1,0:T(8,128)(2,1)S(1)}) custom-call(f32[1,4096]{1,0:T(1,128)S(1)} %get-tuple-element.24.gain_ref, f32[2,24,128]{2,1,0:T(8,128)S(1)} %get-tuple-element.25.frames_ref, bf16[2,24,4096]{2,1,0:T(8,128)(2,1)S(1)} %get-tuple-element.26.batches_ref, ...), custom_call_target="tpu_custom_call" | custom-call | flops 452984832 | bytes 1572864 | tf_op jit(solution)/shard_map/begin/pallas_call | solution.py:379
  6.2 1.2 %collective-permute-done.1.values_ref.refs_3_ = bf16[768,512]{1,0:T(8,128)(2,1)S(1)} collective-permute-done((bf16[768,512]{1,0:T(8,128)(2,1)}, bf16[768,512]{1,0:T(8,128)(2,1)S(1)}, u32[]{:S(2)}, u32[]{:S(2)}) %collective-permute-start.1) | collective-permute-done | bytes 786464 | tf_op jit(solution)/shard_map/ppermute | solution.py:52
  7.4 0.0 collective-permute-done.keys_ref.refs_2_
  7.4 1.6 %finish.1 = (bf16[208,128]{1,0:T(8,128)(2,1)S(1)}, bf16[208,128]{1,0:T(8,128)(2,1)S(1)}, bf16[208,128]{1,0:T(8,128)(2,1)S(1)}, bf16[208,128]{1,0:T(8,128)(2,1)S(1)}) custom-call(f32[2,24,128]{2,1,0:T(8,128)S(1)} %get-tuple-element.25.frames_ref, bf16[768,128]{1,0:T(8,128)(2,1)S(1)} %get-tuple-element.31.queries_ref, ...), custom_call_target="tpu_custom_call" | custom-call | flops 452984832 | bytes 1572864 | tf_op jit(solution)/shard_map/finish/pallas_call | solution.py:427
  9.0 2.8 %collective-permute-start.2 = (bf16[208,128]{1,0:T(8,128)(2,1)S(1)}, bf16[208,128]{1,0:T(8,128)(2,1)S(1)}, u32[]{:S(2)}, u32[]{:S(2)}) collective-permute-start(bf16[208,128]{1,0:T(8,128)(2,1)S(1)} %get-tuple-element.35), channel_id=1, source_target_pairs={{0,4},{1,5},{2,6},{3,7},{4,8},{5,9},{6,10},{7,11},{8,12},{9,13},{1... | collective-permute-start | bytes 159752 | tf_op jit(solution)/shard_map/ppermute | solution.py:67
  11.8 2.6 %collective-permute-start.3 = (bf16[208,128]{1,0:T(8,128)(2,1)S(1)}, bf16[208,128]{1,0:T(8,128)(2,1)S(1)}, u32[]{:S(2)}, u32[]{:S(2)}) collective-permute-start(bf16[208,128]{1,0:T(8,128)(2,1)S(1)} %get-tuple-element.36), channel_id=1, source_target_pairs={{0,8},{1,9},{2,10},{3,11},{4,12},{5,13},{6,14},{7,15},{8,0},{9,1},... | collective-permute-start | bytes 159752 | tf_op jit(solution)/shard_map/ppermute | solution.py:67
  14.4 1.3 %collective-permute-start.4 = (bf16[208,128]{1,0:T(8,128)(2,1)S(1)}, bf16[208,128]{1,0:T(8,128)(2,1)S(1)}, u32[]{:S(2)}, u32[]{:S(2)}) collective-permute-start(bf16[208,128]{1,0:T(8,128)(2,1)S(1)} %get-tuple-element.37), channel_id=1, source_target_pairs={{0,12},{1,13},{2,14},{3,15},{4,0},{5,1},{6,2},{7,3},{8,4},{9,5},{1... | collective-permute-start | bytes 159752 | tf_op jit(solution)/shard_map/ppermute | solution.py:67
  15.7 0.5 collective-permute-done.2.refs_1_
  16.3 2.3 %collective-permute-done.3.refs_2_ = bf16[208,128]{1,0:T(8,128)(2,1)S(1)} collective-permute-done((bf16[208,128]{1,0:T(8,128)(2,1)S(1)}, bf16[208,128]{1,0:T(8,128)(2,1)S(1)}, u32[]{:S(2)}, u32[]{:S(2)}) %collective-permute-start.3) | collective-permute-done | bytes 53280 | tf_op jit(solution)/shard_map/ppermute | solution.py:67
  18.5 0.4 collective-permute-done.4.refs_3_
  18.9 0.3 merge.2
  19.2 4.4 %collective-permute-start.6 = (bf16[208,128]{1,0:T(8,128)(2,1)S(1)}, bf16[208,128]{1,0:T(8,128)(2,1)S(1)}, u32[]{:S(2)}, u32[]{:S(2)}) collective-permute-start(bf16[208,128]{1,0:T(8,128)(2,1)S(1)} %merge.2), channel_id=1, source_target_pairs={{0,18},{1,19},{2,16},{3,17},{4,22},{5,23},{6,20},{7,21},{8,26},{9,... | collective-permute-start | bytes 159752 | tf_op jit(solution)/shard_map/ppermute | solution.py:79
  23.5 1.3 %collective-permute-start.5 = (bf16[208,128]{1,0:T(8,128)(2,1)S(1)}, bf16[208,128]{1,0:T(8,128)(2,1)S(1)}, u32[]{:S(2)}, u32[]{:S(2)}) collective-permute-start(bf16[208,128]{1,0:T(8,128)(2,1)S(1)} %merge.2), channel_id=1, source_target_pairs={{0,16},{1,17},{2,18},{3,19},{4,20},{5,21},{6,22},{7,23},{8,24},{9,... | collective-permute-start | bytes 159752 | tf_op jit(solution)/shard_map/ppermute | solution.py:79
  24.8 1.3 %collective-permute-start.7 = (bf16[24,1024]{1,0:T(8,128)(2,1)S(1)}, bf16[24,1024]{1,0:T(8,128)(2,1)S(1)}, u32[]{:S(2)}, u32[]{:S(2)}) collective-permute-start(bf16[24,1024]{1,0:T(8,128)(2,1)S(1)} %get-tuple-element.38), channel_id=1, source_target_pairs={{0,16},{1,17},{2,18},{3,19},{4,20},{5,21},{6,22},{7,23},{8,24},{9,... | collective-permute-start | bytes 147464 | tf_op jit(solution)/shard_map/ppermute | solution.py:79
  26.1 1.7 %collective-permute-done.7.share_ref = bf16[24,1024]{1,0:T(8,128)(2,1)S(1)} collective-permute-done((bf16[24,1024]{1,0:T(8,128)(2,1)S(1)}, bf16[24,1024]{1,0:T(8,128)(2,1)S(1)}, u32[]{:S(2)}, u32[]{:S(2)}) %collective-permute-start.7) | collective-permute-done | bytes 49184 | tf_op jit(solution)/shard_map/ppermute | solution.py:79
  27.8 0.0 collective-permute-done.5.one_ref
  27.9 0.2 combine.2.refs_4_.handed_ref
  28.1 2.8 %collective-permute-start.10 = (bf16[24,1024]{1,0:T(8,128)(2,1)S(1)}, bf16[24,1024]{1,0:T(8,128)(2,1)S(1)}, u32[]{:S(2)}, u32[]{:S(2)}) collective-permute-start(bf16[24,1024]{1,0:T(8,128)(2,1)S(1)} %combine.2.refs_4_.handed_ref), channel_id=1, source_target_pairs={{0,12},{1,13},{2,14},{3,15},{4,0},{5,1},{6,2},{7,3},{8,4},{9,5},{1... | collective-permute-start | bytes 147464 | tf_op jit(solution)/shard_map/ppermute | solution.py:67
  30.9 0.0 collective-permute-start.9
  30.9 0.6 %collective-permute-start.8 = (bf16[24,1024]{1,0:T(8,128)(2,1)S(1)}, bf16[24,1024]{1,0:T(8,128)(2,1)S(1)}, u32[]{:S(2)}, u32[]{:S(2)}) collective-permute-start(bf16[24,1024]{1,0:T(8,128)(2,1)S(1)} %combine.2.refs_4_.handed_ref), channel_id=1, source_target_pairs={{0,4},{1,5},{2,6},{3,7},{4,8},{5,9},{6,10},{7,11},{8,12},{9,13},{1... | collective-permute-start | bytes 147464 | tf_op jit(solution)/shard_map/ppermute | solution.py:67
  31.6 1.1 %collective-permute-done.10.refs_7_ = bf16[24,1024]{1,0:T(8,128)(2,1)S(1)} collective-permute-done((bf16[24,1024]{1,0:T(8,128)(2,1)S(1)}, bf16[24,1024]{1,0:T(8,128)(2,1)S(1)}, u32[]{:S(2)}, u32[]{:S(2)}) %collective-permute-start.10) | collective-permute-done | bytes 49184 | tf_op jit(solution)/shard_map/ppermute | solution.py:67
  32.7 3.2 %collective-permute-done.9.refs_6_ = bf16[24,1024]{1,0:T(8,128)(2,1)S(1)} collective-permute-done((bf16[24,1024]{1,0:T(8,128)(2,1)S(1)}, bf16[24,1024]{1,0:T(8,128)(2,1)S(1)}, u32[]{:S(2)}, u32[]{:S(2)}) %collective-permute-start.9) | collective-permute-done | bytes 49184 | tf_op jit(solution)/shard_map/ppermute | solution.py:67
  35.9 0.9 %collective-permute-done.8.refs_5_ = bf16[24,1024]{1,0:T(8,128)(2,1)S(1)} collective-permute-done((bf16[24,1024]{1,0:T(8,128)(2,1)S(1)}, bf16[24,1024]{1,0:T(8,128)(2,1)S(1)}, u32[]{:S(2)}, u32[]{:S(2)}) %collective-permute-start.8) | collective-permute-done | bytes 49184 | tf_op jit(solution)/shard_map/ppermute | solution.py:67
  36.8 2.2 %partials.1 = (bf16[208,128]{1,0:T(8,128)(2,1)S(1)}, bf16[208,128]{1,0:T(8,128)(2,1)S(1)}, bf16[208,128]{1,0:T(8,128)(2,1)S(1)}, bf16[208,128]{1,0:T(8,128)(2,1)S(1)}) custom-call(f32[1,4096]{1,0:T(1,128)S(1)} %get-tuple-element.24.gain_ref, f32[2,24,128]{2,1,0:T(8,128)S(1)} %get-tuple-element.25.frames_ref, ...), custom_call_target="tpu_custom_call" | custom-call | flops 905969664 | bytes 3145728 | tf_op jit(solution)/shard_map/partials/pallas_call | solution.py:473
  39.0 0.1 collective-permute-start.11
  39.0 1.2 %collective-permute-start.12 = (bf16[208,128]{1,0:T(8,128)(2,1)S(1)}, bf16[208,128]{1,0:T(8,128)(2,1)S(1)}, u32[]{:S(2)}, u32[]{:S(2)}) collective-permute-start(bf16[208,128]{1,0:T(8,128)(2,1)S(1)} %get-tuple-element.41), channel_id=1, source_target_pairs={{0,8},{1,9},{2,10},{3,11},{4,12},{5,13},{6,14},{7,15},{8,0},{9,1},... | collective-permute-start | bytes 159752 | tf_op jit(solution)/shard_map/ppermute | solution.py:67
  40.2 2.8 %collective-permute-start.13 = (bf16[208,128]{1,0:T(8,128)(2,1)S(1)}, bf16[208,128]{1,0:T(8,128)(2,1)S(1)}, u32[]{:S(2)}, u32[]{:S(2)}) collective-permute-start(bf16[208,128]{1,0:T(8,128)(2,1)S(1)} %get-tuple-element.42), channel_id=1, source_target_pairs={{0,12},{1,13},{2,14},{3,15},{4,0},{5,1},{6,2},{7,3},{8,4},{9,5},{1... | collective-permute-start | bytes 159752 | tf_op jit(solution)/shard_map/ppermute | solution.py:67
  43.0 1.9 %collective-permute-done.11.refs_1_ = bf16[208,128]{1,0:T(8,128)(2,1)S(1)} collective-permute-done((bf16[208,128]{1,0:T(8,128)(2,1)S(1)}, bf16[208,128]{1,0:T(8,128)(2,1)S(1)}, u32[]{:S(2)}, u32[]{:S(2)}) %collective-permute-start.11) | collective-permute-done | bytes 53280 | tf_op jit(solution)/shard_map/ppermute | solution.py:67
  45.0 0.0 collective-permute-done.12.refs_2_
  45.0 0.6 collective-permute-done.13.refs_3_
  45.5 0.3 merge.3.one_ref
  45.8 0.6 %collective-permute-start.14 = (bf16[208,128]{1,0:T(8,128)(2,1)S(1)}, bf16[208,128]{1,0:T(8,128)(2,1)S(1)}, u32[]{:S(2)}, u32[]{:S(2)}) collective-permute-start(bf16[208,128]{1,0:T(8,128)(2,1)S(1)} %merge.3.one_ref), channel_id=1, source_target_pairs={{0,2},{1,3},{2,0},{3,1},{4,6},{5,7},{6,4},{7,5},{8,10},{9,11},{10,... | collective-permute-start | bytes 159752 | tf_op jit(solution)/shard_map/ppermute | solution.py:61
  46.4 3.6 %collective-permute-done.14.two_ref = bf16[208,128]{1,0:T(8,128)(2,1)S(1)} collective-permute-done((bf16[208,128]{1,0:T(8,128)(2,1)S(1)}, bf16[208,128]{1,0:T(8,128)(2,1)S(1)}, u32[]{:S(2)}, u32[]{:S(2)}) %collective-permute-start.14) | collective-permute-done | bytes 53280 | tf_op jit(solution)/shard_map/ppermute | solution.py:61
  50.0 0.2 combine.3.refs_0_
  50.2 3.5 %collective-permute-start.17 = (bf16[24,1024]{1,0:T(8,128)(2,1)S(1)}, bf16[24,1024]{1,0:T(8,128)(2,1)S(1)}, u32[]{:S(2)}, u32[]{:S(2)}) collective-permute-start(bf16[24,1024]{1,0:T(8,128)(2,1)S(1)} %combine.3.refs_0_), channel_id=1, source_target_pairs={{0,12},{1,13},{2,14},{3,15},{4,0},{5,1},{6,2},{7,3},{8,4},{9,5},{1... | collective-permute-start | bytes 147464 | tf_op jit(solution)/shard_map/ppermute | solution.py:67
  53.7 0.0 collective-permute-start.16
  53.8 0.6 collective-permute-start.15
  54.4 0.0 collective-permute-start.18
  54.4 1.1 %collective-permute-done.17.refs_3_ = bf16[24,1024]{1,0:T(8,128)(2,1)S(1)} collective-permute-done((bf16[24,1024]{1,0:T(8,128)(2,1)S(1)}, bf16[24,1024]{1,0:T(8,128)(2,1)S(1)}, u32[]{:S(2)}, u32[]{:S(2)}) %collective-permute-start.17) | collective-permute-done | bytes 49184 | tf_op jit(solution)/shard_map/ppermute | solution.py:67
  55.5 3.2 %collective-permute-done.16.refs_2_ = bf16[24,1024]{1,0:T(8,128)(2,1)S(1)} collective-permute-done((bf16[24,1024]{1,0:T(8,128)(2,1)S(1)}, bf16[24,1024]{1,0:T(8,128)(2,1)S(1)}, u32[]{:S(2)}, u32[]{:S(2)}) %collective-permute-start.16) | collective-permute-done | bytes 49184 | tf_op jit(solution)/shard_map/ppermute | solution.py:67
  58.7 0.9 %collective-permute-done.15.refs_1_ = bf16[24,1024]{1,0:T(8,128)(2,1)S(1)} collective-permute-done((bf16[24,1024]{1,0:T(8,128)(2,1)S(1)}, bf16[24,1024]{1,0:T(8,128)(2,1)S(1)}, u32[]{:S(2)}, u32[]{:S(2)}) %collective-permute-start.15) | collective-permute-done | bytes 49184 | tf_op jit(solution)/shard_map/ppermute | solution.py:67
  59.7 0.3 collective-permute-done.20.refs_6_
  60.0 0.9 %collective-permute-done.19.refs_5_ = bf16[24,1024]{1,0:T(8,128)(2,1)S(1)} collective-permute-done((bf16[24,1024]{1,0:T(8,128)(2,1)S(1)}, bf16[24,1024]{1,0:T(8,128)(2,1)S(1)}, u32[]{:S(2)}, u32[]{:S(2)}) %collective-permute-start.19) | collective-permute-done | bytes 49184 | tf_op jit(solution)/shard_map/ppermute | solution.py:52
  60.9 0.8 %assemble.1 = bf16[24,8192]{1,0:T(8,128)(2,1)} custom-call(bf16[24,1024]{1,0:T(8,128)(2,1)S(1)} %combine.3.refs_0_, bf16[24,1024]{1,0:T(8,128)(2,1)S(1)} %collective-permute-done.15.refs_1_, bf16[24,1024]{1,0:T(8,128)(2,1)S(1)} %collective-permute-done.16.refs_2_, bf16[24,1024]{1,0:T(8,128)(2,1)S(1)} %collective-permute-done.17.refs_3_, ...), custom_call_target="tpu_custom_call" | custom-call | tf_op jit(solution)/shard_map/assemble/pallas_call | solution.py:553
  (6 shorter events, 0.0 us)
Async XLA Ops:
  2.1 5.3 %collective-permute-start = (bf16[784,512]{1,0:T(8,128)(2,1)}, bf16[784,512]{1,0:T(8,128)(2,1)S(1)}, u32[]{:S(2)}, u32[]{:S(2)}) collective-permute-start(bf16[784,512]{1,0:T(8,128)(2,1)} %get-tuple-element.29), channel_id=1, source_target_pairs={{0,1},{1,0},{2,3},{3,2},{4,5},{5,4},{6,7},{7,6},{8,9},{9,8},{10,11... | collective-permute-start | bytes 2408456 | tf_op jit(solution)/shard_map/ppermute | solution.py:52
  4.9 2.6 %collective-permute-start.1 = (bf16[768,512]{1,0:T(8,128)(2,1)}, bf16[768,512]{1,0:T(8,128)(2,1)S(1)}, u32[]{:S(2)}, u32[]{:S(2)}) collective-permute-start(bf16[768,512]{1,0:T(8,128)(2,1)} %get-tuple-element.30), channel_id=1, source_target_pairs={{0,1},{1,0},{2,3},{3,2},{4,5},{5,4},{6,7},{7,6},{8,9},{9,8},{10,11... | collective-permute-start | bytes 2359304 | tf_op jit(solution)/shard_map/ppermute | solution.py:52
  9.0 7.2 %collective-permute-start.2 = (bf16[208,128]{1,0:T(8,128)(2,1)S(1)}, bf16[208,128]{1,0:T(8,128)(2,1)S(1)}, u32[]{:S(2)}, u32[]{:S(2)}) collective-permute-start(bf16[208,128]{1,0:T(8,128)(2,1)S(1)} %get-tuple-element.35), channel_id=1, source_target_pairs={{0,4},{1,5},{2,6},{3,7},{4,8},{5,9},{6,10},{7,11},{8,12},{9,13},{1... | collective-permute-start | bytes 159752 | tf_op jit(solution)/shard_map/ppermute | solution.py:67
  11.8 6.7 %collective-permute-start.3 = (bf16[208,128]{1,0:T(8,128)(2,1)S(1)}, bf16[208,128]{1,0:T(8,128)(2,1)S(1)}, u32[]{:S(2)}, u32[]{:S(2)}) collective-permute-start(bf16[208,128]{1,0:T(8,128)(2,1)S(1)} %get-tuple-element.36), channel_id=1, source_target_pairs={{0,8},{1,9},{2,10},{3,11},{4,12},{5,13},{6,14},{7,15},{8,0},{9,1},... | collective-permute-start | bytes 159752 | tf_op jit(solution)/shard_map/ppermute | solution.py:67
  14.4 4.5 %collective-permute-start.4 = (bf16[208,128]{1,0:T(8,128)(2,1)S(1)}, bf16[208,128]{1,0:T(8,128)(2,1)S(1)}, u32[]{:S(2)}, u32[]{:S(2)}) collective-permute-start(bf16[208,128]{1,0:T(8,128)(2,1)S(1)} %get-tuple-element.37), channel_id=1, source_target_pairs={{0,12},{1,13},{2,14},{3,15},{4,0},{5,1},{6,2},{7,3},{8,4},{9,5},{1... | collective-permute-start | bytes 159752 | tf_op jit(solution)/shard_map/ppermute | solution.py:67
  19.2 8.7 %collective-permute-start.6 = (bf16[208,128]{1,0:T(8,128)(2,1)S(1)}, bf16[208,128]{1,0:T(8,128)(2,1)S(1)}, u32[]{:S(2)}, u32[]{:S(2)}) collective-permute-start(bf16[208,128]{1,0:T(8,128)(2,1)S(1)} %merge.2), channel_id=1, source_target_pairs={{0,18},{1,19},{2,16},{3,17},{4,22},{5,23},{6,20},{7,21},{8,26},{9,... | collective-permute-start | bytes 159752 | tf_op jit(solution)/shard_map/ppermute | solution.py:79
  23.5 4.3 %collective-permute-start.5 = (bf16[208,128]{1,0:T(8,128)(2,1)S(1)}, bf16[208,128]{1,0:T(8,128)(2,1)S(1)}, u32[]{:S(2)}, u32[]{:S(2)}) collective-permute-start(bf16[208,128]{1,0:T(8,128)(2,1)S(1)} %merge.2), channel_id=1, source_target_pairs={{0,16},{1,17},{2,18},{3,19},{4,20},{5,21},{6,22},{7,23},{8,24},{9,... | collective-permute-start | bytes 159752 | tf_op jit(solution)/shard_map/ppermute | solution.py:79
  24.8 3.0 %collective-permute-start.7 = (bf16[24,1024]{1,0:T(8,128)(2,1)S(1)}, bf16[24,1024]{1,0:T(8,128)(2,1)S(1)}, u32[]{:S(2)}, u32[]{:S(2)}) collective-permute-start(bf16[24,1024]{1,0:T(8,128)(2,1)S(1)} %get-tuple-element.38), channel_id=1, source_target_pairs={{0,16},{1,17},{2,18},{3,19},{4,20},{5,21},{6,22},{7,23},{8,24},{9,... | collective-permute-start | bytes 147464 | tf_op jit(solution)/shard_map/ppermute | solution.py:79
  28.1 4.6 %collective-permute-start.10 = (bf16[24,1024]{1,0:T(8,128)(2,1)S(1)}, bf16[24,1024]{1,0:T(8,128)(2,1)S(1)}, u32[]{:S(2)}, u32[]{:S(2)}) collective-permute-start(bf16[24,1024]{1,0:T(8,128)(2,1)S(1)} %combine.2.refs_4_.handed_ref), channel_id=1, source_target_pairs={{0,12},{1,13},{2,14},{3,15},{4,0},{5,1},{6,2},{7,3},{8,4},{9,5},{1... | collective-permute-start | bytes 147464 | tf_op jit(solution)/shard_map/ppermute | solution.py:67
  30.9 5.0 %collective-permute-start.9 = (bf16[24,1024]{1,0:T(8,128)(2,1)S(1)}, bf16[24,1024]{1,0:T(8,128)(2,1)S(1)}, u32[]{:S(2)}, u32[]{:S(2)}) collective-permute-start(bf16[24,1024]{1,0:T(8,128)(2,1)S(1)} %combine.2.refs_4_.handed_ref), channel_id=1, source_target_pairs={{0,8},{1,9},{2,10},{3,11},{4,12},{5,13},{6,14},{7,15},{8,0},{9,1},... | collective-permute-start | bytes 147464 | tf_op jit(solution)/shard_map/ppermute | solution.py:67
  30.9 5.9 %collective-permute-start.8 = (bf16[24,1024]{1,0:T(8,128)(2,1)S(1)}, bf16[24,1024]{1,0:T(8,128)(2,1)S(1)}, u32[]{:S(2)}, u32[]{:S(2)}) collective-permute-start(bf16[24,1024]{1,0:T(8,128)(2,1)S(1)} %combine.2.refs_4_.handed_ref), channel_id=1, source_target_pairs={{0,4},{1,5},{2,6},{3,7},{4,8},{5,9},{6,10},{7,11},{8,12},{9,13},{1... | collective-permute-start | bytes 147464 | tf_op jit(solution)/shard_map/ppermute | solution.py:67
  39.0 6.0 %collective-permute-start.11 = (bf16[208,128]{1,0:T(8,128)(2,1)S(1)}, bf16[208,128]{1,0:T(8,128)(2,1)S(1)}, u32[]{:S(2)}, u32[]{:S(2)}) collective-permute-start(bf16[208,128]{1,0:T(8,128)(2,1)S(1)} %get-tuple-element.40), channel_id=1, source_target_pairs={{0,4},{1,5},{2,6},{3,7},{4,8},{5,9},{6,10},{7,11},{8,12},{9,13},{1... | collective-permute-start | bytes 159752 | tf_op jit(solution)/shard_map/ppermute | solution.py:67
  39.0 5.9 %collective-permute-start.12 = (bf16[208,128]{1,0:T(8,128)(2,1)S(1)}, bf16[208,128]{1,0:T(8,128)(2,1)S(1)}, u32[]{:S(2)}, u32[]{:S(2)}) collective-permute-start(bf16[208,128]{1,0:T(8,128)(2,1)S(1)} %get-tuple-element.41), channel_id=1, source_target_pairs={{0,8},{1,9},{2,10},{3,11},{4,12},{5,13},{6,14},{7,15},{8,0},{9,1},... | collective-permute-start | bytes 159752 | tf_op jit(solution)/shard_map/ppermute | solution.py:67
  40.2 5.3 %collective-permute-start.13 = (bf16[208,128]{1,0:T(8,128)(2,1)S(1)}, bf16[208,128]{1,0:T(8,128)(2,1)S(1)}, u32[]{:S(2)}, u32[]{:S(2)}) collective-permute-start(bf16[208,128]{1,0:T(8,128)(2,1)S(1)} %get-tuple-element.42), channel_id=1, source_target_pairs={{0,12},{1,13},{2,14},{3,15},{4,0},{5,1},{6,2},{7,3},{8,4},{9,5},{1... | collective-permute-start | bytes 159752 | tf_op jit(solution)/shard_map/ppermute | solution.py:67
  45.8 4.2 %collective-permute-start.14 = (bf16[208,128]{1,0:T(8,128)(2,1)S(1)}, bf16[208,128]{1,0:T(8,128)(2,1)S(1)}, u32[]{:S(2)}, u32[]{:S(2)}) collective-permute-start(bf16[208,128]{1,0:T(8,128)(2,1)S(1)} %merge.3.one_ref), channel_id=1, source_target_pairs={{0,2},{1,3},{2,0},{3,1},{4,6},{5,7},{6,4},{7,5},{8,10},{9,11},{10,... | collective-permute-start | bytes 159752 | tf_op jit(solution)/shard_map/ppermute | solution.py:61
  50.2 5.3 %collective-permute-start.17 = (bf16[24,1024]{1,0:T(8,128)(2,1)S(1)}, bf16[24,1024]{1,0:T(8,128)(2,1)S(1)}, u32[]{:S(2)}, u32[]{:S(2)}) collective-permute-start(bf16[24,1024]{1,0:T(8,128)(2,1)S(1)} %combine.3.refs_0_), channel_id=1, source_target_pairs={{0,12},{1,13},{2,14},{3,15},{4,0},{5,1},{6,2},{7,3},{8,4},{9,5},{1... | collective-permute-start | bytes 147464 | tf_op jit(solution)/shard_map/ppermute | solution.py:67
  53.7 5.0 %collective-permute-start.16 = (bf16[24,1024]{1,0:T(8,128)(2,1)S(1)}, bf16[24,1024]{1,0:T(8,128)(2,1)S(1)}, u32[]{:S(2)}, u32[]{:S(2)}) collective-permute-start(bf16[24,1024]{1,0:T(8,128)(2,1)S(1)} %combine.3.refs_0_), channel_id=1, source_target_pairs={{0,8},{1,9},{2,10},{3,11},{4,12},{5,13},{6,14},{7,15},{8,0},{9,1},... | collective-permute-start | bytes 147464 | tf_op jit(solution)/shard_map/ppermute | solution.py:67
  53.8 5.9 %collective-permute-start.15 = (bf16[24,1024]{1,0:T(8,128)(2,1)S(1)}, bf16[24,1024]{1,0:T(8,128)(2,1)S(1)}, u32[]{:S(2)}, u32[]{:S(2)}) collective-permute-start(bf16[24,1024]{1,0:T(8,128)(2,1)S(1)} %combine.3.refs_0_), channel_id=1, source_target_pairs={{0,4},{1,5},{2,6},{3,7},{4,8},{5,9},{6,10},{7,11},{8,12},{9,13},{1... | collective-permute-start | bytes 147464 | tf_op jit(solution)/shard_map/ppermute | solution.py:67
  54.4 5.3 %collective-permute-start.18 = (bf16[24,1024]{1,0:T(8,128)(2,1)S(1)}, bf16[24,1024]{1,0:T(8,128)(2,1)S(1)}, u32[]{:S(2)}, u32[]{:S(2)}) collective-permute-start(bf16[24,1024]{1,0:T(8,128)(2,1)S(1)} %combine.3.refs_0_), channel_id=1, source_target_pairs={{0,1},{1,0},{2,3},{3,2},{4,5},{5,4},{6,7},{7,6},{8,9},{9,8},{10,11... | collective-permute-start | bytes 147464 | tf_op jit(solution)/shard_map/ppermute | solution.py:52
  55.5 4.2 %collective-permute-start.21 = (bf16[24,1024]{1,0:T(8,128)(2,1)S(1)}, bf16[24,1024]{1,0:T(8,128)(2,1)S(1)}, u32[]{:S(2)}, u32[]{:S(2)}) collective-permute-start(bf16[24,1024]{1,0:T(8,128)(2,1)S(1)} %collective-permute-done.17.refs_3_), channel_id=1, source_target_pairs={{0,1},{1,0},{2,3},{3,2},{4,5},{5,4},{6,7},{7,6},{8,9},{9,8},{10,11... | collective-permute-start | bytes 147464 | tf_op jit(solution)/shard_map/ppermute | solution.py:52
  58.7 1.2 %collective-permute-start.20 = (bf16[24,1024]{1,0:T(8,128)(2,1)S(1)}, bf16[24,1024]{1,0:T(8,128)(2,1)S(1)}, u32[]{:S(2)}, u32[]{:S(2)}) collective-permute-start(bf16[24,1024]{1,0:T(8,128)(2,1)S(1)} %collective-permute-done.16.refs_2_), channel_id=1, source_target_pairs={{0,1},{1,0},{2,3},{3,2},{4,5},{5,4},{6,7},{7,6},{8,9},{9,8},{10,11... | collective-permute-start | bytes 147464 | tf_op jit(solution)/shard_map/ppermute | solution.py:52
  59.6 1.2 %collective-permute-start.19 = (bf16[24,1024]{1,0:T(8,128)(2,1)S(1)}, bf16[24,1024]{1,0:T(8,128)(2,1)S(1)}, u32[]{:S(2)}, u32[]{:S(2)}) collective-permute-start(bf16[24,1024]{1,0:T(8,128)(2,1)S(1)} %collective-permute-done.15.refs_1_), channel_id=1, source_target_pairs={{0,1},{1,0},{2,3},{3,2},{4,5},{5,4},{6,7},{7,6},{8,9},{9,8},{10,11... | collective-permute-start | bytes 147464 | tf_op jit(solution)/shard_map/ppermute | solution.py:52
